TPU v7x, 32 devices: a whole 2x2x4 slice. The times are simulated.
32 devices in a mesh: dp: 16 (over z, y, core), tensor: 2 (over x).
Axes of the slice: x: 2, y: 2, z: 4, core: 2. Of those that a mesh axis runs over, the one named last changes fastest.
Arguments:
- tokens: bfloat16 [12800, 512], P('dp'), may hold values from -6 to 6
- memory: bfloat16 [131072, 512], P('dp'), may hold values from -6 to 6
- mem_lengths: int32 [32, 4], P('dp'), may hold values from 1 to 1200, 4096 in all within a row
- key_pad: int32 [32, 4096], P('dp'), may hold values 0 or 1
- query_embed: float32 [100, 512], replicated, may hold values from -5 to 5
- self_wq: bfloat16 [512, 512], P(None, 'tensor'), may hold values from -0.25 to 0.25
- self_bq: float32 [512], P('tensor'), may hold values from -3 to 3
- self_wk: bfloat16 [512, 512], P(None, 'tensor'), may hold values from -0.25 to 0.25
- self_wv: bfloat16 [512, 512], P(None, 'tensor'), may hold values from -0.25 to 0.25
- self_bv: float32 [512], P('tensor'), may hold values from -3 to 3
- self_wo: bfloat16 [512, 512], P('tensor'), may hold values from -0.5 to 0.5
- self_bo: float32 [512], replicated, may hold values from -3 to 3
- norm1_gain: float32 [512], replicated, may hold values from 0.5 to 1.5
- norm1_bias: float32 [512], replicated, may hold values from -2 to 2
- cross_wq: bfloat16 [512, 512], P(None, 'tensor'), may hold values from -0.25 to 0.25
- cross_bq: float32 [512], P('tensor'), may hold values from -3 to 3
- cross_wk: bfloat16 [512, 512], P(None, 'tensor'), may hold values from -0.25 to 0.25
- cross_wv: bfloat16 [512, 512], P(None, 'tensor'), may hold values from -0.25 to 0.25
- cross_bv: float32 [512], P('tensor'), may hold values from -3 to 3
- cross_wo: bfloat16 [512, 512], P('tensor'), may hold values from -1 to 1
- cross_bo: float32 [512], replicated, may hold values from -3 to 3
- norm2_gain: float32 [512], replicated, may hold values from 0.5 to 1.5
- norm2_bias: float32 [512], replicated, may hold values from -2 to 2
- ffn_w1: bfloat16 [512, 3200], P(None, 'tensor'), may hold values from -0.25 to 0.25
- ffn_b1: float32 [3200], P('tensor'), may hold values from -3 to 3
- ffn_w2: bfloat16 [3200, 512], P('tensor'), may hold values from -0.109375 to 0.109375
- ffn_b2: float32 [512], replicated, may hold values from -3 to 3
- norm3_gain: float32 [512], replicated, may hold values from 0.5 to 1.5
- norm3_bias: float32 [512], replicated, may hold values from -2 to 2
- cotangent: bfloat16 [12800, 512], P('dp'), may hold values from -6 to 6
Outputs:
- layer_out: bfloat16 [12800, 512], P('dp')
- grad_tokens: float32 [12800, 512], P('dp')
- grad_memory: float32 [131072, 512], P('dp')
- grad_query_embed: float32 [100, 512], replicated
- grad_self_wq: float32 [512, 512], P(None, 'tensor')
- grad_self_bq: float32 [512], P('tensor')
- grad_self_wk: float32 [512, 512], P(None, 'tensor')
- grad_self_wv: float32 [512, 512], P(None, 'tensor')
- grad_self_bv: float32 [512], P('tensor')
- grad_self_wo: float32 [512, 512], P('tensor')
- grad_self_bo: float32 [512], replicated
- grad_norm1_gain: float32 [512], replicated
- grad_norm1_bias: float32 [512], replicated
- grad_cross_wq: float32 [512, 512], P(None, 'tensor')
- grad_cross_bq: float32 [512], P('tensor')
- grad_cross_wk: float32 [512, 512], P(None, 'tensor')
- grad_cross_wv: float32 [512, 512], P(None, 'tensor')
- grad_cross_bv: float32 [512], P('tensor')
- grad_cross_wo: float32 [512, 512], P('tensor')
- grad_cross_bo: float32 [512], replicated
- grad_norm2_gain: float32 [512], replicated
- grad_norm2_bias: float32 [512], replicated
- grad_ffn_w1: float32 [512, 3200], P(None, 'tensor')
- grad_ffn_b1: float32 [3200], P('tensor')
- grad_ffn_w2: float32 [3200, 512], P('tensor')
- grad_ffn_b2: float32 [512], replicated
- grad_norm3_gain: float32 [512], replicated
- grad_norm3_bias: float32 [512], replicated
Inputs may be any that keep to these rules, and one draw needn't show every extreme that they name: `mem_lengths`: the 4 lengths of a row sum to 4096.
All inputs are finite; a program needn't handle non-finite values. No bound on the sum of `key_pad` on one device may be relied on, other than what follows from the above.
Results may differ from a plain program's by a relative error of at most 0.028.
The roundings to bfloat16 on the way count: a program that leaves them out, or rounds other values in their place, can miss the bound.
Values may be sent and summed in bfloat16 or wider, within the bound.
No kernel may reach another device: no remote copies, remote signals or barrier semaphores. Data moves between devices by JAX's collectives and lax.ppermute only.
A program may use at most 256 MiB of HBM per device.

v0:
```python
import math

import jax
import jax.numpy as jnp
from jax import lax
from jax.sharding import PartitionSpec as P

HEAD = 64
SPAN = 100


def matmul(left, right):
    return jnp.dot(left, right, preferred_element_type=jnp.float32)


def outer_product(left, right):
    return lax.dot_general(
        left, right, (((0,), (0,)), ((), ())), preferred_element_type=jnp.float32
    )


def times_transposed(left, right):
    return lax.dot_general(
        left, right, (((1,), (1,)), ((), ())), preferred_element_type=jnp.float32
    )


def column_sums(matrix):
    return jnp.sum(matrix.astype(jnp.float32), axis=0)


def layer_norm(value_in, norm_gain, norm_shift):
    center = value_in - jnp.mean(value_in, axis=-1, keepdims=True)
    spread = jnp.mean(center * center, axis=-1, keepdims=True)
    return center * lax.rsqrt(spread + 1e-05) * norm_gain + norm_shift


def smooth_act(pre_act):
    return (
        0.5
        * pre_act
        * (
            1.0
            + jnp.tanh(
                math.sqrt(2.0 / math.pi) * (pre_act + 0.044715 * pre_act * pre_act * pre_act)
            )
        )
    )


def memory_layout(lengths_row, slot_count):
    item_ends = jnp.cumsum(lengths_row)
    starts = item_ends - lengths_row
    slot_index = jnp.arange(slot_count, dtype=jnp.int32)
    slot_owner = jnp.sum((slot_index[:, None] >= item_ends[None, :]).astype(jnp.int32), axis=1)
    chosen = slot_owner[:, None] == jnp.arange(lengths_row.shape[0], dtype=jnp.int32)[None, :]
    start_of = jnp.sum(jnp.where(chosen, starts[None, :], 0), axis=1)
    return (slot_owner, slot_index - start_of)


def cross_allowed(lengths_row, pad_row, query_count):
    slot_owner, slot_place = memory_layout(lengths_row, pad_row.shape[0])
    is_valid = (pad_row > 0) | (slot_place == 0)
    query_item = jnp.arange(query_count, dtype=jnp.int32) // SPAN
    return (query_item[:, None] == slot_owner[None, :]) & is_valid[None, :]


def sinusoid(places, feature_dim):
    freq_index = jnp.arange(feature_dim // 2, dtype=jnp.float32)
    freq_rates = jnp.exp(freq_index * (-2.0 * math.log(10000.0) / feature_dim))
    angles = places.astype(jnp.float32)[:, None] * freq_rates[None, :]
    return jnp.stack([jnp.sin(angles), jnp.cos(angles)], axis=-1).reshape(
        places.shape[0], feature_dim
    )


def scores_of(queries, keys_in, allowed):
    scores = jnp.einsum(
        "qhe,khe->hqk", queries, keys_in, preferred_element_type=jnp.float32
    ) / math.sqrt(HEAD)
    return jnp.where(allowed[None], scores, -1000000000.0)


def attend_forward(queries, keys_in, values_in, allowed):
    scores = scores_of(queries, keys_in, allowed)
    largest = jnp.max(scores, axis=-1, keepdims=True)
    expo_terms = jnp.exp(scores - largest)
    denominator = jnp.sum(expo_terms, axis=-1, keepdims=True)
    weights_low = (expo_terms / denominator).astype(jnp.bfloat16)
    mixed_out = jnp.einsum(
        "hqk,khe->qhe", weights_low, values_in, preferred_element_type=jnp.float32
    )
    return (mixed_out.astype(jnp.bfloat16), largest, denominator)


def attend_backward(queries, keys_in, values_in, allowed, largest, denominator, grad_mixed):
    scores = scores_of(queries, keys_in, allowed)
    exact_probs = jnp.exp(scores - largest) / denominator
    weights_low = exact_probs.astype(jnp.bfloat16)
    grad_values = jnp.einsum(
        "hqk,qhe->khe", weights_low, grad_mixed, preferred_element_type=jnp.float32
    )
    grad_weights = jnp.einsum(
        "qhe,khe->hqk", grad_mixed, values_in, preferred_element_type=jnp.float32
    )
    row_inner = jnp.sum(grad_weights * exact_probs, axis=-1, keepdims=True)
    grad_scores = (exact_probs * (grad_weights - row_inner)).astype(jnp.bfloat16)
    grad_queries = jnp.einsum(
        "hqk,khe->qhe", grad_scores, keys_in, preferred_element_type=jnp.float32
    ) / math.sqrt(HEAD)
    grad_keys = jnp.einsum(
        "hqk,qhe->khe", grad_scores, queries, preferred_element_type=jnp.float32
    ) / math.sqrt(HEAD)
    return (
        grad_queries.astype(jnp.bfloat16),
        grad_keys.astype(jnp.bfloat16),
        grad_values.astype(jnp.bfloat16),
    )


def body(
    tokens,
    memory,
    mem_lengths,
    key_pad,
    query_embed,
    self_wq,
    self_bq,
    self_wk,
    self_wv,
    self_bv,
    self_wo,
    self_bo,
    norm1_gain,
    norm1_bias,
    cross_wq,
    cross_bq,
    cross_wk,
    cross_wv,
    cross_bv,
    cross_wo,
    cross_bo,
    norm2_gain,
    norm2_bias,
    ffn_w1,
    ffn_b1,
    ffn_w2,
    ffn_b2,
    norm3_gain,
    norm3_bias,
    cotangent,
):
    row_count = mem_lengths.shape[0]
    token_count = tokens.shape[0]
    query_count = token_count // row_count
    slot_count = memory.shape[0] // row_count
    feature_dim = tokens.shape[1]
    local_width = self_wq.shape[1]
    local_heads = local_width // HEAD
    block_count = token_count // SPAN
    query_pos = jnp.tile(query_embed, (block_count, 1))
    tokens_wide = tokens.astype(jnp.float32)
    square = jnp.ones((SPAN, SPAN), dtype=bool)

    def branch_total(partial_sum):
        return lax.psum(partial_sum, "tensor")

    def input_total(partial_sum):
        return lax.psum(partial_sum, "tensor")

    def to_items(matrix):
        return matrix.reshape(block_count, SPAN, local_heads, HEAD)

    def to_rows(matrix, length):
        return matrix.reshape(row_count, length, local_heads, HEAD)

    def self_block(queries, keys_in, values_in):
        return attend_forward(queries, keys_in, values_in, square)

    def self_block_back(queries, keys_in, values_in, largest, denominator, grad_mixed):
        return attend_backward(
            queries, keys_in, values_in, square, largest, denominator, grad_mixed
        )

    def cross_row(row_data):
        queries, keys_in, values_in, lengths_row, pad_row = row_data
        allowed = cross_allowed(lengths_row, pad_row, queries.shape[0])
        return attend_forward(queries, keys_in, values_in, allowed)

    def cross_row_back(row_data):
        queries, keys_in, values_in, lengths_row, pad_row, largest, denominator, grad_mixed = (
            row_data
        )
        allowed = cross_allowed(lengths_row, pad_row, queries.shape[0])
        return attend_backward(
            queries, keys_in, values_in, allowed, largest, denominator, grad_mixed
        )

    def places_of(lengths_row):
        return memory_layout(lengths_row, slot_count)[1]

    shared_in = (tokens_wide + query_pos).astype(jnp.bfloat16)
    self_query = (matmul(shared_in, self_wq) + self_bq).astype(jnp.bfloat16)
    self_keys = matmul(shared_in, self_wk).astype(jnp.bfloat16)
    self_values = (matmul(tokens, self_wv) + self_bv).astype(jnp.bfloat16)
    self_mix, self_largest, self_denom = jax.vmap(self_block)(
        to_items(self_query), to_items(self_keys), to_items(self_values)
    )
    self_mix = self_mix.reshape(token_count, local_width)
    resid_one = tokens_wide + (branch_total(matmul(self_mix, self_wo)) + self_bo)
    normed_one, pull_one = jax.vjp(layer_norm, resid_one, norm1_gain, norm1_bias)
    memory_pos = sinusoid(jax.vmap(places_of)(mem_lengths).reshape(-1), feature_dim)
    cross_in = (normed_one + query_pos).astype(jnp.bfloat16)
    memory_in = (memory.astype(jnp.float32) + memory_pos).astype(jnp.bfloat16)
    cross_query = (matmul(cross_in, cross_wq) + cross_bq).astype(jnp.bfloat16)
    cross_keys = matmul(memory_in, cross_wk).astype(jnp.bfloat16)
    cross_values = (matmul(memory, cross_wv) + cross_bv).astype(jnp.bfloat16)
    cross_mix, cross_largest, cross_denom = lax.map(
        cross_row,
        (
            to_rows(cross_query, query_count),
            to_rows(cross_keys, slot_count),
            to_rows(cross_values, slot_count),
            mem_lengths,
            key_pad,
        ),
    )
    cross_mix = cross_mix.reshape(token_count, local_width)
    resid_two = normed_one + (branch_total(matmul(cross_mix, cross_wo)) + cross_bo)
    normed_two, pull_two = jax.vjp(layer_norm, resid_two, norm2_gain, norm2_bias)
    ffn_input = normed_two.astype(jnp.bfloat16)
    pre_act = matmul(ffn_input, ffn_w1) + ffn_b1
    hidden_wide, pull_act = jax.vjp(smooth_act, pre_act)
    hidden = hidden_wide.astype(jnp.bfloat16)
    resid_three = normed_two + (branch_total(matmul(hidden, ffn_w2)) + ffn_b2)
    normed_three, pull_three = jax.vjp(layer_norm, resid_three, norm3_gain, norm3_bias)
    layer_out = normed_three.astype(jnp.bfloat16)
    grad_three, grad_norm3_gain, grad_norm3_bias = pull_three(cotangent.astype(jnp.float32))
    low_three = grad_three.astype(jnp.bfloat16)
    grad_ffn_b2 = column_sums(low_three)
    grad_ffn_w2 = outer_product(hidden, low_three)
    (grad_pre,) = pull_act(times_transposed(low_three, ffn_w2))
    low_pre = grad_pre.astype(jnp.bfloat16)
    grad_ffn_b1 = column_sums(low_pre)
    grad_ffn_w1 = outer_product(ffn_input, low_pre)
    grad_two, grad_norm2_gain, grad_norm2_bias = pull_two(
        grad_three + input_total(times_transposed(low_pre, ffn_w1))
    )
    low_two = grad_two.astype(jnp.bfloat16)
    grad_cross_bo = column_sums(low_two)
    grad_cross_wo = outer_product(cross_mix, low_two)
    grad_cross_mix = times_transposed(low_two, cross_wo).astype(jnp.bfloat16)
    grad_cross_query, grad_cross_keys, grad_cross_values = lax.map(
        cross_row_back,
        (
            to_rows(cross_query, query_count),
            to_rows(cross_keys, slot_count),
            to_rows(cross_values, slot_count),
            mem_lengths,
            key_pad,
            cross_largest,
            cross_denom,
            to_rows(grad_cross_mix, query_count),
        ),
    )
    grad_cross_query = grad_cross_query.reshape(token_count, local_width)
    grad_cross_keys = grad_cross_keys.reshape(row_count * slot_count, local_width)
    grad_cross_values = grad_cross_values.reshape(row_count * slot_count, local_width)
    grad_cross_bq = column_sums(grad_cross_query)
    grad_cross_wq = outer_product(cross_in, grad_cross_query)
    grad_cross_wk = outer_product(memory_in, grad_cross_keys)
    grad_cross_wv = outer_product(memory, grad_cross_values)
    grad_cross_bv = column_sums(grad_cross_values)
    memory_part = times_transposed(grad_cross_keys, cross_wk) + times_transposed(
        grad_cross_values, cross_wv
    )
    grad_memory = lax.psum(memory_part.astype(jnp.bfloat16), "tensor").astype(jnp.float32)
    grad_cross_in = input_total(times_transposed(grad_cross_query, cross_wq))
    grad_one, grad_norm1_gain, grad_norm1_bias = pull_one(grad_two + grad_cross_in)
    low_one = grad_one.astype(jnp.bfloat16)
    grad_self_bo = column_sums(low_one)
    grad_self_wo = outer_product(self_mix, low_one)
    grad_self_mix = times_transposed(low_one, self_wo).astype(jnp.bfloat16)
    grad_self_query, grad_self_keys, grad_self_values = jax.vmap(self_block_back)(
        to_items(self_query),
        to_items(self_keys),
        to_items(self_values),
        self_largest,
        self_denom,
        to_items(grad_self_mix),
    )
    grad_self_query = grad_self_query.reshape(token_count, local_width)
    grad_self_keys = grad_self_keys.reshape(token_count, local_width)
    grad_self_values = grad_self_values.reshape(token_count, local_width)
    grad_self_bq = column_sums(grad_self_query)
    grad_self_wq = outer_product(shared_in, grad_self_query)
    grad_self_wk = outer_product(shared_in, grad_self_keys)
    grad_self_wv = outer_product(tokens, grad_self_values)
    grad_self_bv = column_sums(grad_self_values)
    shared_part = times_transposed(grad_self_query, self_wq) + times_transposed(
        grad_self_keys, self_wk
    )
    position_part = jnp.sum(shared_part.reshape(block_count, SPAN, feature_dim), axis=0)
    input_part = shared_part + times_transposed(grad_self_values, self_wv)
    input_sum, position_sum = (
        lax.psum(input_part.astype(jnp.bfloat16), "tensor").astype(jnp.float32),
        lax.psum(position_part.astype(jnp.bfloat16), "tensor").astype(jnp.float32),
    )
    grad_tokens = grad_one + input_sum
    grad_query_embed = position_sum + jnp.sum(
        grad_cross_in.reshape(block_count, SPAN, feature_dim), axis=0
    )
    (
        grad_query_embed,
        grad_self_wq,
        grad_self_bq,
        grad_self_wk,
        grad_self_wv,
        grad_self_bv,
        grad_self_wo,
        grad_self_bo,
        grad_norm1_gain,
        grad_norm1_bias,
        grad_cross_wq,
        grad_cross_bq,
        grad_cross_wk,
        grad_cross_wv,
        grad_cross_bv,
        grad_cross_wo,
        grad_cross_bo,
        grad_norm2_gain,
        grad_norm2_bias,
        grad_ffn_w1,
        grad_ffn_b1,
        grad_ffn_w2,
        grad_ffn_b2,
        grad_norm3_gain,
        grad_norm3_bias,
    ) = (
        lax.psum(grad_query_embed.astype(jnp.bfloat16), "dp").astype(jnp.float32),
        lax.psum(grad_self_wq.astype(jnp.bfloat16), "dp").astype(jnp.float32),
        lax.psum(grad_self_bq.astype(jnp.bfloat16), "dp").astype(jnp.float32),
        lax.psum(grad_self_wk.astype(jnp.bfloat16), "dp").astype(jnp.float32),
        lax.psum(grad_self_wv.astype(jnp.bfloat16), "dp").astype(jnp.float32),
        lax.psum(grad_self_bv.astype(jnp.bfloat16), "dp").astype(jnp.float32),
        lax.psum(grad_self_wo.astype(jnp.bfloat16), "dp").astype(jnp.float32),
        lax.psum(grad_self_bo.astype(jnp.bfloat16), "dp").astype(jnp.float32),
        lax.psum(grad_norm1_gain.astype(jnp.bfloat16), "dp").astype(jnp.float32),
        lax.psum(grad_norm1_bias.astype(jnp.bfloat16), "dp").astype(jnp.float32),
        lax.psum(grad_cross_wq.astype(jnp.bfloat16), "dp").astype(jnp.float32),
        lax.psum(grad_cross_bq.astype(jnp.bfloat16), "dp").astype(jnp.float32),
        lax.psum(grad_cross_wk.astype(jnp.bfloat16), "dp").astype(jnp.float32),
        lax.psum(grad_cross_wv.astype(jnp.bfloat16), "dp").astype(jnp.float32),
        lax.psum(grad_cross_bv.astype(jnp.bfloat16), "dp").astype(jnp.float32),
        lax.psum(grad_cross_wo.astype(jnp.bfloat16), "dp").astype(jnp.float32),
        lax.psum(grad_cross_bo.astype(jnp.bfloat16), "dp").astype(jnp.float32),
        lax.psum(grad_norm2_gain.astype(jnp.bfloat16), "dp").astype(jnp.float32),
        lax.psum(grad_norm2_bias.astype(jnp.bfloat16), "dp").astype(jnp.float32),
        lax.psum(grad_ffn_w1.astype(jnp.bfloat16), "dp").astype(jnp.float32),
        lax.psum(grad_ffn_b1.astype(jnp.bfloat16), "dp").astype(jnp.float32),
        lax.psum(grad_ffn_w2.astype(jnp.bfloat16), "dp").astype(jnp.float32),
        lax.psum(grad_ffn_b2.astype(jnp.bfloat16), "dp").astype(jnp.float32),
        lax.psum(grad_norm3_gain.astype(jnp.bfloat16), "dp").astype(jnp.float32),
        lax.psum(grad_norm3_bias.astype(jnp.bfloat16), "dp").astype(jnp.float32),
    )
    return (
        layer_out,
        grad_tokens,
        grad_memory,
        grad_query_embed,
        grad_self_wq,
        grad_self_bq,
        grad_self_wk,
        grad_self_wv,
        grad_self_bv,
        grad_self_wo,
        grad_self_bo,
        grad_norm1_gain,
        grad_norm1_bias,
        grad_cross_wq,
        grad_cross_bq,
        grad_cross_wk,
        grad_cross_wv,
        grad_cross_bv,
        grad_cross_wo,
        grad_cross_bo,
        grad_norm2_gain,
        grad_norm2_bias,
        grad_ffn_w1,
        grad_ffn_b1,
        grad_ffn_w2,
        grad_ffn_b2,
        grad_norm3_gain,
        grad_norm3_bias,
    )


def solution(mesh):
    return jax.shard_map(
        body,
        mesh=mesh,
        in_specs=(
            P("dp", None),
            P("dp", None),
            P("dp", None),
            P("dp", None),
            P(),
            P(None, "tensor"),
            P("tensor"),
            P(None, "tensor"),
            P(None, "tensor"),
            P("tensor"),
            P("tensor", None),
            P(),
            P(),
            P(),
            P(None, "tensor"),
            P("tensor"),
            P(None, "tensor"),
            P(None, "tensor"),
            P("tensor"),
            P("tensor", None),
            P(),
            P(),
            P(),
            P(None, "tensor"),
            P("tensor"),
            P("tensor", None),
            P(),
            P(),
            P(),
            P("dp", None),
        ),
        out_specs=(
            P("dp", None),
            P("dp", None),
            P("dp", None),
            P(),
            P(None, "tensor"),
            P("tensor"),
            P(None, "tensor"),
            P(None, "tensor"),
            P("tensor"),
            P("tensor", None),
            P(),
            P(),
            P(),
            P(None, "tensor"),
            P("tensor"),
            P(None, "tensor"),
            P(None, "tensor"),
            P("tensor"),
            P("tensor", None),
            P(),
            P(),
            P(),
            P(None, "tensor"),
            P("tensor"),
            P("tensor", None),
            P(),
            P(),
            P(),
        ),
        check_vma=False,
    )
```

profile of v0, /device:TPU:0, one launch (start us, length us, event | category | flops | bytes accessed | tf_op | source)
XLA Modules:
  0.0 1180.8 jit_solution(12925456234667355802)
XLA Ops:
  46.0 29.9 %multiply_sine_fusion = (f32[8192,256,1]{1,0,2:T(8,128)S(1)}, f32[8192,256,1]{1,0,2:T(8,128)S(1)}) fusion(f32[256]{0:T(256)S(1)} %multiply_exponential_fusion, f32[8192]{0:T(1024)S(1)} %bitcast.282), kind=kLoop, calls=%fused_computation.100 | loop fusion | flops 2097152 | bytes 16811008 | tf_op jit(solution)/shard_map/sin | solution.py:72
  82.1 25.4 %copy.166 = f32[8192,256,2]{0,2,1:T(2,128)} copy(f32[8192,256,2]{1,0,2:T(8,128)} %pad_maximum_fusion) | data formatting | bytes 33554432 | tf_op jit(solution)/shard_map/stack | solution.py:72
  107.6 20.5 %reshape.551 = f32[8192,512]{0,1:T(8,128)} reshape(f32[8192,256,2]{0,2,1:T(2,128)} %copy.166) | data formatting | bytes 33554432 | tf_op jit(solution)/shard_map/reshape | solution.py:72
  140.1 13.3 %convolution_convert_fusion = bf16[8192,256]{1,0:T(8,128)(2,1)} fusion(bf16[512,256]{1,0:T(8,128)(2,1)S(1)} %copy-done.45, f32[8192,512]{0,1:T(8,128)} %reshape.551, bf16[8192,512]{0,1:T(8,128)(2,1)} %copy.165), kind=kOutput, calls=%fused_computation.101 | convolution fusion | flops 2162163712 | bytes 29622272 | tf_op jit(solution)/shard_map/dot_general | solution.py:13
  153.4 12.9 %reshape.570 = bf16[2,4096,4,64]{3,2,1,0:T(4,128)(2,1)} reshape(bf16[8192,256]{1,0:T(8,128)(2,1)} %convolution_convert_fusion) | data formatting | bytes 8388608 | tf_op jit(solution)/shard_map/reshape | solution.py:175
  186.9 12.9 %reshape.568 = bf16[2,4096,4,64]{3,2,1,0:T(4,128)(2,1)} reshape(bf16[8192,256]{1,0:T(8,128)(2,1)} %fusion.81) | data formatting | bytes 8388608 | tf_op jit(solution)/shard_map/reshape | solution.py:175
  219.7 82.4 %while.32 = (s32[]{:T(128)}, bf16[2,400,4,64]{1,3,2,0:T(8,128)(2,1)}, f32[2,4,400,1]{2,1,3,0:T(4,128)S(1)}, f32[2,4,400,1]{2,1,3,0:T(4,128)}, bf16[2,4096,4,64]{...) while((s32[]{:T(128)}, ...), condition=%wide.region_14.15_spmd, body=%wide.region_8.14_spmd.sunk | while | flops 1759850496 | bytes 91731112 | solution.py:218
  247.0 13.9 %fusion.230 = bf16[2,400,4,64]{1,3,2,0:T(8,128)(2,1)} fusion(bf16[2,400,4,64]{1,3,2,0:T(8,128)(2,1)} %get-tuple-element.775, s32[]{:T(128)} %get-tuple-element.774, f32[4,400,4096]{2,1,0:T(8,128)} %get-tuple-element.743, f32[4,400]{1,0:T(4,128)S(1)} %fusion.229, f32[4,400]{1,0:T(4,128)S(1)} %get-tuple-element.744, ...), kind=kOutput, calls=%fused_computation.14.clone.1 | convolution fusion | flops 871731200 | bytes 30225920 | tf_op jit(solution)/shard_map/while/body/eval_jaxpr/hqk,khe->qhe/dot_general | solution.py:90
  288.2 13.9 %fusion.230 = bf16[2,400,4,64]{1,3,2,0:T(8,128)(2,1)} fusion(bf16[2,400,4,64]{1,3,2,0:T(8,128)(2,1)} %get-tuple-element.775, s32[]{:T(128)} %get-tuple-element.774, f32[4,400,4096]{2,1,0:T(8,128)} %get-tuple-element.743, f32[4,400]{1,0:T(4,128)S(1)} %fusion.229, f32[4,400]{1,0:T(4,128)S(1)} %get-tuple-element.744, ...), kind=kOutput, calls=%fused_computation.14.clone.1 | convolution fusion | flops 871731200 | bytes 30225920 | tf_op jit(solution)/shard_map/while/body/eval_jaxpr/hqk,khe->qhe/dot_general | solution.py:90
  308.1 55.4 %all-reduce.13.cloned.1.call-done = f32[800,512]{1,0:T(8,128)} async-done(((f32[800,512]{1,0:T(8,128)}), f32[800,512]{1,0:T(8,128)}) %all-reduce.13.cloned.1.call-update) | async-done | bytes 1638416 | tf_op jit(solution)/shard_map/psum | solution.py:166
  375.5 53.0 %all-reduce.15.cloned.1.call-done = f32[800,512]{1,0:T(8,128)} async-done(((f32[800,512]{1,0:T(8,128)}), f32[800,512]{1,0:T(8,128)}) %all-reduce.15.cloned.1.call-update) | async-done | bytes 1638416 | tf_op jit(solution)/shard_map/psum | solution.py:166
  449.7 53.0 %all-reduce.17.cloned.1.call-done = f32[800,512]{1,0:T(8,128)} async-done(((f32[800,512]{1,0:T(8,128)}), f32[800,512]{1,0:T(8,128)}) %all-reduce.17.cloned.1.call-update) | async-done | bytes 1638416 | tf_op jit(solution)/shard_map/psum | solution.py:169
  509.7 171.8 %while.33 = (s32[]{:T(128)}, bf16[2,400,4,64]{1,3,2,0:T(8,128)(2,1)S(1)}, bf16[2,4096,4,64]{1,3,2,0:T(8,128)(2,1)}, bf16[2,4096,4,64]{1,3,2,0:T(8,128)(2,1)}, bf...) while((s32[]{:T(128)}, ...), condition=%wide.region_31.32_spmd, body=%wide.region_26.31_spmd.sunk | while | flops 4266575360 | bytes 314611712 | solution.py:253
  513.6 14.3 %exponential_divide_fusion.5 = f32[4,400,4096]{2,1,0:T(8,128)} fusion(f32[4,400]{1,0:T(4,128)S(1)} %get-tuple-element.759, f32[4,400]{1,0:T(4,128)S(1)} %get-tuple-element.760, pred[400,4096]{1,0:T(8,128)(4,1)S(1)} %compare_and_fusion.5, bf16[2,4096,4,64]{1,3,2,0:T(8,128)(2,1)} %get-tuple-element.828, s32[]{:T(128)} %get-tuple-element.810, ...), kind=kOutput, calls=%fused_computation.41.clone.1 | convolution fusion | flops 865075200 | bytes 30229504 | tf_op jit(solution)/shard_map/while/body/eval_jaxpr/qhe,khe->hqk/dot_general | solution.py:78
  527.9 21.4 %multiply_reduce_fusion.11 = (f32[4,400]{1,0:T(4,128)S(1)}, f32[4,400,4096]{2,1,0:T(8,128)}) fusion(f32[4,400,4096]{2,1,0:T(8,128)} %exponential_divide_fusion.5, bf16[2,4096,4,64]{1,3,2,0:T(8,128)(2,1)} %get-tuple-element.835, s32[]{:T(128)} %get-tuple-element.810, bf16[2,400,4,64]{1,3,2,0:T(8,128)(2,1)S(1)} %get-tuple-element.834), kind=kOutput, calls=%fused_computation.40.clone.1 | convolution fusion | flops 851966400 | bytes 54795520 | tf_op jit(solution)/shard_map/while/body/eval_jaxpr/qhe,khe->hqk/dot_general | solution.py:103
  549.3 17.3 %multiply_convert_fusion.4 = bf16[4,400,4096]{2,1,0:T(8,128)(2,1)S(1)} fusion(f32[4,400,4096]{2,1,0:T(8,128)} %exponential_divide_fusion.5, f32[4,400,4096]{2,1,0:T(8,128)} %get-tuple-element.761, f32[4,400]{1,0:T(4,128)S(1)} %get-tuple-element.762), kind=kLoop, calls=%fused_computation.39.clone.1 | loop fusion | flops 19660800 | bytes 65542400 | tf_op jit(solution)/shard_map/while/body/eval_jaxpr/convert_element_type | solution.py:107
  599.2 14.3 %exponential_divide_fusion.5 = f32[4,400,4096]{2,1,0:T(8,128)} fusion(f32[4,400]{1,0:T(4,128)S(1)} %get-tuple-element.759, f32[4,400]{1,0:T(4,128)S(1)} %get-tuple-element.760, pred[400,4096]{1,0:T(8,128)(4,1)S(1)} %compare_and_fusion.5, bf16[2,4096,4,64]{1,3,2,0:T(8,128)(2,1)} %get-tuple-element.828, s32[]{:T(128)} %get-tuple-element.810, ...), kind=kOutput, calls=%fused_computation.41.clone.1 | convolution fusion | flops 865075200 | bytes 30229504 | tf_op jit(solution)/shard_map/while/body/eval_jaxpr/qhe,khe->hqk/dot_general | solution.py:78
  613.5 21.4 %multiply_reduce_fusion.11 = (f32[4,400]{1,0:T(4,128)S(1)}, f32[4,400,4096]{2,1,0:T(8,128)}) fusion(f32[4,400,4096]{2,1,0:T(8,128)} %exponential_divide_fusion.5, bf16[2,4096,4,64]{1,3,2,0:T(8,128)(2,1)} %get-tuple-element.835, s32[]{:T(128)} %get-tuple-element.810, bf16[2,400,4,64]{1,3,2,0:T(8,128)(2,1)S(1)} %get-tuple-element.834), kind=kOutput, calls=%fused_computation.40.clone.1 | convolution fusion | flops 851966400 | bytes 54795520 | tf_op jit(solution)/shard_map/while/body/eval_jaxpr/qhe,khe->hqk/dot_general | solution.py:103
  634.9 17.3 %multiply_convert_fusion.4 = bf16[4,400,4096]{2,1,0:T(8,128)(2,1)S(1)} fusion(f32[4,400,4096]{2,1,0:T(8,128)} %exponential_divide_fusion.5, f32[4,400,4096]{2,1,0:T(8,128)} %get-tuple-element.761, f32[4,400]{1,0:T(4,128)S(1)} %get-tuple-element.762), kind=kLoop, calls=%fused_computation.39.clone.1 | loop fusion | flops 19660800 | bytes 65542400 | tf_op jit(solution)/shard_map/while/body/eval_jaxpr/convert_element_type | solution.py:107
  719.2 13.4 %add_convert_fusion = bf16[8192,512]{1,0:T(8,128)(2,1)} fusion(f32[8192,512]{1,0:T(8,128)} %fusion.137, bf16[8192,256]{0,1:T(8,128)(2,1)} %bitcast.274, bf16[512,256]{1,0:T(8,128)(2,1)S(1)} %copy-done.61), kind=kOutput, calls=%fused_computation.97 | convolution fusion | flops 2155872256 | bytes 29622272 | tf_op jit(solution)/shard_map/dot_general | solution.py:23
  732.6 39.3 %all-reduce.19.cloned.1.call-done = f32[800,512]{1,0:T(8,128)} async-done(((f32[800,512]{1,0:T(8,128)}), f32[800,512]{1,0:T(8,128)}) %all-reduce.19.cloned.1.call-update) | async-done | bytes 1638416 | tf_op jit(solution)/shard_map/psum | solution.py:169
  836.7 182.6 %all-reduce.23.cloned.1.call-done = (bf16[100,512]{1,0:T(8,128)(2,1)}, bf16[800,512]{1,0:T(8,128)(2,1)}, bf16[8192,512]{1,0:T(8,128)(2,1)}) async-done(((bf16[100,512]{1,0:T(8,128)(2,1)}, bf16[800,512]{1,0:T(8,128)(2,1)}, bf16[8192,512]{1,0:T(8,128)(2,1)}), (bf16[100,512]{1,0:T(8,128)(2,1)}, bf16[800,512]{1,0:T(8,128)(2,1)}, bf16[8192,512]{1,0:T(8,128)(2,1)})) %all-reduce.23.cloned.1.call-update) | async-done | bytes 9310224 | tf_op jit(solution)/shard_map/psum | solution.py:307
  1025.7 64.1 %all-reduce = (bf16[256]{0:T(256)(128)(2,1)S(1)}, bf16[256]{0:T(256)(128)(2,1)S(1)}, bf16[512]{0:T(512)(128)(2,1)S(1)}, bf16[512]{0:T(512)(128)(2,1)S(1)}, bf16[...) all-reduce(bf16[256]{0:T(256)(128)(2,1)S(1)} %reduce_sum.466, ...), channel_id=1, replica_groups=mesh['dp'=16,'tensor'=2] {'dp'}, use_global_device_ids=true, to_apply=%region_44.45 | all-reduce | flops 7232 | bytes 28928 | tf_op jit(solution)/shard_map/psum | solution.py:342
  1111.5 48.4 %all-reduce.21.cloned.1.call-done = (bf16[512,256]{0,1:T(8,128)(2,1)}, bf16[512,256]{0,1:T(8,128)(2,1)}, bf16[100,512]{1,0:T(8,128)(2,1)}, bf16[512,256]{1,0:T(8...) async-done(((bf16[512,256]{0,1:T(8,128)(2,1)}, ...) | async-done | bytes 5476368 | tf_op jit(solution)/shard_map/psum | solution.py:344
  (478 shorter events, 406.2 us)
Async XLA Ops:
  7.2 358.7 %copy-start = (bf16[512,1600]{0,1:T(8,128)(2,1)S(1)}, bf16[512,1600]{0,1:T(8,128)(2,1)}, u32[]{:S(2)}) copy-start(bf16[512,1600]{0,1:T(8,128)(2,1)} %param.57) | copy-start | bytes 4915204
  7.2 205.4 %all-reduce.11.cloned.1.call-start = ((), (), s32[]{:S(2)}) async-start(), calls=%async_computation | async-start | bytes 3276800 | tf_op jit(solution)/shard_map/psum | solution.py:166
  45.4 318.0 %all-reduce.13.cloned.1.call-start = ((), (), s32[]{:S(2)}) async-start(), calls=%async_computation.1 | async-start | bytes 3276800 | tf_op jit(solution)/shard_map/psum | solution.py:166
  304.9 58.6 %copy-start.4 = (f32[800,512]{1,0:T(8,128)S(1)}, f32[800,512]{1,0:T(8,128)}, u32[]{:S(2)}) copy-start(f32[800,512]{1,0:T(8,128)} %copy-done.3) | copy-start | bytes 4915204
  304.9 58.6 %copy-start.77 = (f32[800]{0:T(1024)S(1)}, f32[800]{0:T(1024)}, u32[]{:S(2)}) copy-start(f32[800]{0:T(1024)} %copy-done.76) | copy-start | bytes 9604
  304.9 58.6 %copy-start.83 = (f32[800]{0:T(1024)S(1)}, f32[800]{0:T(1024)}, u32[]{:S(2)}) copy-start(f32[800]{0:T(1024)} %copy-done.82) | copy-start | bytes 9604
  304.9 58.6 %copy-start.96 = (f32[512]{0:T(512)S(1)}, f32[512]{0:T(512)}, u32[]{:S(2)}) copy-start(f32[512]{0:T(512)} %param.46) | copy-start | bytes 6148
  307.6 58.3 %copy-start.98 = (f32[512]{0:T(512)S(1)}, f32[512]{0:T(512)}, u32[]{:S(2)}) copy-start(f32[512]{0:T(512)} %param.55) | copy-start | bytes 6148
  307.6 120.9 %all-reduce.15.cloned.1.call-start = ((), (), s32[]{:S(2)}) async-start(), calls=%async_computation.2 | async-start | bytes 3276800 | tf_op jit(solution)/shard_map/psum | solution.py:166
  365.5 140.1 %copy-start.85 = (f32[800]{0:T(1024)}, f32[800]{0:T(1024)S(1)}, u32[]{:S(2)}) copy-start(f32[800]{0:T(1024)S(1)} %broadcast_multiply_fusion.1) | copy-start | bytes 9604
  365.9 139.7 %copy-start.87 = (f32[800]{0:T(1024)}, f32[800]{0:T(1024)S(1)}, u32[]{:S(2)}) copy-start(f32[800]{0:T(1024)S(1)} %fusion.113) | copy-start | bytes 9604
  375.4 53.1 %copy-start.8 = (f32[800,512]{1,0:T(8,128)S(1)}, f32[800,512]{1,0:T(8,128)}, u32[]{:S(2)}) copy-start(f32[800,512]{1,0:T(8,128)} %copy-done.7) | copy-start | bytes 4915204
  375.4 127.3 %all-reduce.17.cloned.1.call-start = ((), (), s32[]{:S(2)}) async-start(), calls=%async_computation.3 | async-start | bytes 3276800 | tf_op jit(solution)/shard_map/psum | solution.py:169
  449.6 53.1 %copy-start.17 = (f32[800,512]{1,0:T(8,128)S(1)}, f32[800,512]{1,0:T(8,128)}, u32[]{:S(2)}) copy-start(f32[800,512]{1,0:T(8,128)} %copy-done.16) | copy-start | bytes 4915204
  449.6 322.4 %all-reduce.19.cloned.1.call-start = ((), (), s32[]{:S(2)}) async-start(), calls=%async_computation.4 | async-start | bytes 3276800 | tf_op jit(solution)/shard_map/psum | solution.py:169
  718.9 300.4 %all-reduce.23.cloned.1.call-start = ((), (), s32[]{:S(2)}) async-start(), calls=%async_computation.6 | async-start | bytes 18628608 | tf_op jit(solution)/shard_map/psum | solution.py:307
  719.2 52.8 %copy-start.5 = (f32[800,512]{1,0:T(8,128)S(1)}, f32[800,512]{1,0:T(8,128)}, u32[]{:S(2)}) copy-start(f32[800,512]{1,0:T(8,128)} %copy-done.3) | copy-start | bytes 4915204
  719.2 52.8 %copy-start.15 = (f32[800,512]{1,0:T(8,128)S(1)}, f32[800,512]{1,0:T(8,128)}, u32[]{:S(2)}) copy-start(f32[800,512]{1,0:T(8,128)} %copy-done.14) | copy-start | bytes 4915204
  719.2 52.8 %copy-start.78 = (f32[800]{0:T(1024)S(1)}, f32[800]{0:T(1024)}, u32[]{:S(2)}) copy-start(f32[800]{0:T(1024)} %copy-done.76) | copy-start | bytes 9604
  719.2 52.8 %copy-start.84 = (f32[800]{0:T(1024)S(1)}, f32[800]{0:T(1024)}, u32[]{:S(2)}) copy-start(f32[800]{0:T(1024)} %copy-done.82) | copy-start | bytes 9604
  719.2 52.8 %copy-start.94 = (f32[800]{0:T(1024)S(1)}, f32[800]{0:T(1024)}, u32[]{:S(2)}) copy-start(f32[800]{0:T(1024)} %copy-done.93) | copy-start | bytes 9604
  719.2 52.8 %copy-start.97 = (f32[512]{0:T(512)S(1)}, f32[512]{0:T(512)}, u32[]{:S(2)}) copy-start(f32[512]{0:T(512)} %param.46) | copy-start | bytes 6148
  732.6 42.2 %copy-start.92 = (f32[800]{0:T(1024)S(1)}, f32[800]{0:T(1024)}, u32[]{:S(2)}) copy-start(f32[800]{0:T(1024)} %copy-done.91) | copy-start | bytes 9604
  800.2 359.7 %all-reduce.21.cloned.1.call-start = ((), (), s32[]{:S(2)}) async-start(), calls=%async_computation.5 | async-start | bytes 10960896 | tf_op jit(solution)/shard_map/psum | solution.py:344
  (116 other events, 476.1 us)
Sparse Core Ops, SparseCore 0:
  45.5 55.6 all-reduce.10
  307.7 55.6 all-reduce.12
  375.6 52.9 all-reduce.14
  449.7 52.9 all-reduce.16
  719.0 52.9 all-reduce.18
  800.3 218.9 all-reduce.22
  1026.3 133.6 all-reduce.20
where the time goes:
time: 1190 us; the launch traced here: 1180 us
  waiting for transfers between devices  432 us (36%)
  matrix products  293 us (25%)
  local copies, waits for them, and re-layouts  205 us (17%)
  other arithmetic  169 us (14%)
  blocking collectives  64.1 us (5%)
  between operations  15.9 us (1%)
    psum x1, waiting for transfers between devices, body(): lax.psum(position_part.astype(jnp.bfloat16), 'tensor').astype(jnp.float32)  183 us
    psum x3, waiting for transfers between devices, branch_total(): return lax.psum(partial_sum, 'tensor')  108 us
    psum x2, waiting for transfers between devices, input_total(): return lax.psum(partial_sum, 'tensor')  92.4 us
    psum x1, blocking collectives, body(): lax.psum(grad_self_bq.astype(jnp.bfloat16), 'dp').astype(jnp.float32)  64.1 us
    dot_general x4, matrix products, scores_of(): jnp.einsum('qhe,khe->hqk', queries, keys_in, preferred_element_type=jnp.f...  53.3 us
    psum x1, waiting for transfers between devices, body(): lax.psum(grad_self_wv.astype(jnp.bfloat16), 'dp').astype(jnp.float32)  48.4 us
    dot_general x3, matrix products, attend_backward(): jnp.einsum('qhe,khe->hqk', grad_mixed, values_in, preferred_element_type=...  43.5 us
    dot_general x10, matrix products, matmul(): return jnp.dot(left, right, preferred_element_type=jnp.float32)  40.4 us
  transfers between devices with their start and end apart: 7, of which 6 were waited for; matrix products, arithmetic and copies ran while one was open for 20% of the time, Pallas kernels for 0%

commit v1 on v0

v1 whole, which is shorter than its diff:
```python
import functools
import math

import jax
import jax.numpy as jnp
import numpy as np
from jax import lax
from jax.experimental import pallas as pl
from jax.experimental.pallas import tpu as pltpu
from jax.sharding import PartitionSpec as P

HEAD = 64
SPAN = 100
LANES = 128
PAIR = 2 * HEAD
TILE = 256
FAR = -1.0e9
BF = jnp.bfloat16
F32 = jnp.float32


def mm(left, right):
    return jnp.dot(left, right, preferred_element_type=F32)


def mm_tn(left, right):
    return lax.dot_general(left, right, (((0,), (0,)), ((), ())), preferred_element_type=F32)


def mm_nt(left, right):
    return lax.dot_general(left, right, (((1,), (1,)), ((), ())), preferred_element_type=F32)


def split3(value):
    top = value.astype(BF)
    rest = value - top.astype(F32)
    middle = rest.astype(BF)
    return top, middle, (rest - middle.astype(F32)).astype(BF)


def iota(shape, dim):
    return lax.broadcasted_iota(jnp.int32, shape, dim)


def keys_values_kernel(
    first_ref, last_ref, starts_ref, ends_ref,
    memory_ref, pad_ref, bounds_ref, sin_ref, cos_ref, local_sin_ref, local_cos_ref, wk_ref, wv_ref, bv_ref,
    memory_in_ref, keys_ref, values_ref, gate_ref,
):
    tiles = pl.num_programs(1)
    row, tile = pl.program_id(0), pl.program_id(1)
    step = row * tiles + tile
    base = tile * TILE
    memory = memory_ref[...]
    local_sin, local_cos = local_sin_ref[...], local_cos_ref[...]
    slots = iota((TILE, 1), 0) + base

    def place(item):
        return sin_ref[0, pl.ds(item, 1), :] * local_cos + cos_ref[0, pl.ds(item, 1), :] * local_sin

    def later(item, held):
        return jnp.where(slots >= starts_ref[row, item], place(item), held)

    first = first_ref[step]
    where_at = lax.fori_loop(first + 1, last_ref[step] + 1, later, place(first))
    memory_in = (memory.astype(F32) + where_at).astype(BF)
    memory_in_ref[...] = memory_in
    keys_ref[...] = mm(memory_in, wk_ref[...]).astype(BF)
    values_ref[...] = (mm(memory, wv_ref[...]) + bv_ref[...]).astype(BF)
    pad = jnp.transpose(jnp.broadcast_to(pad_ref[0].astype(F32), (LANES, TILE)))
    lane_starts, lane_ends = bounds_ref[0, 0:1, :], bounds_ref[0, 1:2, :]
    slot_grid = iota((TILE, LANES), 0) + base
    lane = iota((TILE, LANES), 1)
    mine = (slot_grid >= lane_starts) & (slot_grid < lane_ends)
    is_open = mine & ((pad > 0.0) | (slot_grid == lane_starts))
    items = starts_ref.shape[1]
    gate = jnp.where(lane < items, jnp.where(is_open, 0.0, 1.0), jnp.where(lane < items + 3, 1.0, 0.0))
    gate_ref[...] = gate.astype(BF)


def keys_values(memory, layout, tables, wk, wv, bv):
    rows, tiles = layout["rows"], layout["tiles"]
    feature = memory.shape[1]
    width = wk.shape[1]
    total = memory.shape[0]
    slab = lambda columns: pl.BlockSpec((TILE, columns), lambda r, t, *_: (r * tiles + t, 0))
    whole = lambda array: pl.BlockSpec(array.shape, lambda r, t, *_: (0,) * array.ndim)
    per_tile = lambda array: pl.BlockSpec((1,) + array.shape[1:], lambda r, t, *_: (r * tiles + t, 0, 0))
    return pl.pallas_call(
        keys_values_kernel,
        grid_spec=pltpu.PrefetchScalarGridSpec(
            num_scalar_prefetch=4,
            grid=(rows, tiles),
            in_specs=[
                slab(feature),
                per_tile(layout["pad"]),
                pl.BlockSpec((1,) + layout["bounds"].shape[1:], lambda r, t, *_: (r, 0, 0)),
                per_tile(tables["tile_sin"]),
                per_tile(tables["tile_cos"]),
                whole(tables["local_sin"]),
                whole(tables["local_cos"]),
                whole(wk), whole(wv), whole(bv),
            ],
            out_specs=[slab(feature), slab(width), slab(width), slab(LANES)],
        ),
        out_shape=[
            jax.ShapeDtypeStruct((total, feature), BF),
            jax.ShapeDtypeStruct((total, width), BF),
            jax.ShapeDtypeStruct((total, width), BF),
            jax.ShapeDtypeStruct((total, LANES), BF),
        ],
        compiler_params=pltpu.CompilerParams(vmem_limit_bytes=40 << 20),
        cost_estimate=pl.CostEstimate(flops=4 * total * feature * width, bytes_accessed=total * 4096, transcendentals=0),
        name="keys_values",
    )(
        layout["first"], layout["last"], layout["starts"], layout["ends"],
        memory, layout["pad"], layout["bounds"], tables["tile_sin"], tables["tile_cos"],
        tables["local_sin"], tables["local_cos"], wk, wv, bv,
    )


def block_rows(pair_transposed):
    blank = jnp.zeros((HEAD, pair_transposed.shape[1]), BF)
    upper = jnp.concatenate([pair_transposed[:HEAD], blank], axis=1)
    lower = jnp.concatenate([blank, pair_transposed[HEAD:]], axis=1)
    return jnp.concatenate([upper, lower], axis=0)


def block_columns(pair):
    twice = jnp.concatenate([pair, pair], axis=0)
    same = (iota(twice.shape, 0) < pair.shape[0]) == (iota(twice.shape, 1) < HEAD)
    return jnp.where(same, twice, jnp.zeros_like(twice))


def gate_rows(item, items, closed, added):
    row = iota((LANES, 2 * LANES), 0)
    value = jnp.where(row == item, closed, 0.0)
    if added is not None:
        for place, part in enumerate(split3(added)):
            value = jnp.where(row == items + place, part.astype(F32), value)
    return value.astype(BF)


def cross_forward_kernel(starts_ref, ends_ref, keys_ref, values_ref, gate_ref, qt_ref, mix_ref, lse_ref, right_ref, scores_ref, acc_ref):
    row = pl.program_id(0)
    items = starts_ref.shape[1]
    width = keys_ref.shape[1]
    pairs = width // PAIR

    def one_item(item, carry):
        start, end = starts_ref[row, item], ends_ref[row, item]
        tile_from = start // TILE
        tile_to = (end + (TILE - 1)) // TILE
        closed = gate_rows(item, items, FAR, None)
        for pair in range(pairs):
            right_ref[pair, :PAIR, :] = block_rows(qt_ref[item, pl.ds(pair * PAIR, PAIR), :])
            right_ref[pair, PAIR:, :] = closed
            acc_ref[pair] = jnp.zeros((PAIR, 2 * LANES), F32)

        def score_tile(tile, largest):
            where_at = pl.ds(pl.multiple_of(tile * TILE, TILE), TILE)
            gate = gate_ref[where_at, :]
            out = []
            for pair in range(pairs):
                left = jnp.concatenate([keys_ref[where_at, pair * PAIR : (pair + 1) * PAIR], gate], axis=1)
                scores = mm(left, right_ref[pair])
                scores_ref[tile - tile_from, :, pair * 2 * LANES : (pair + 1) * 2 * LANES] = scores
                out.append(jnp.maximum(largest[pair], jnp.max(scores.reshape(TILE // 8, 8, 2 * LANES), axis=0)))
            return tuple(out)

        lowest = jnp.full((8, 2 * LANES), -3.0e38, F32)
        largest = lax.fori_loop(tile_from, tile_to, score_tile, (lowest,) * pairs)
        largest = [jnp.max(one, axis=0, keepdims=True) for one in largest]

        def mix_tile(tile, sums):
            where_at = pl.ds(pl.multiple_of(tile * TILE, TILE), TILE)
            out = []
            for pair in range(pairs):
                scores = scores_ref[tile - tile_from, :, pair * 2 * LANES : (pair + 1) * 2 * LANES]
                expo = jnp.exp(scores - largest[pair])
                out.append(sums[pair] + jnp.sum(expo.reshape(TILE // 8, 8, 2 * LANES), axis=0))
                values = values_ref[where_at, pair * PAIR : (pair + 1) * PAIR]
                acc_ref[pair] += mm_tn(values, expo.astype(BF))
            return tuple(out)

        sums = lax.fori_loop(tile_from, tile_to, mix_tile, (jnp.zeros((8, 2 * LANES), F32),) * pairs)
        mixed = []
        for pair in range(pairs):
            total = jnp.sum(sums[pair], axis=0, keepdims=True)
            both = acc_ref[pair] / total
            mixed += [both[:HEAD, :LANES], both[HEAD:, LANES:]]
            lse = largest[pair] + jnp.log(total)
            lse_ref[item, 2 * pair : 2 * pair + 1, :] = lse[:, :LANES]
            lse_ref[item, 2 * pair + 1 : 2 * pair + 2, :] = lse[:, LANES:]
        mix_ref[item] = jnp.transpose(jnp.concatenate(mixed, axis=0))
        return carry

    lax.fori_loop(0, items, one_item, 0)


def cross_forward(keys, values, gate, qt, layout):
    rows, items = layout["rows"], layout["items"]
    slots = layout["slots"]
    width = keys.shape[1]
    heads = width // HEAD
    tiles_most = min(slots, -(-layout["longest"] // TILE) * TILE + TILE) // TILE
    by_row = lambda columns: pl.BlockSpec((slots, columns), lambda r, *_: (r, 0))
    by_items = lambda one, two: pl.BlockSpec((items, one, two), lambda r, *_: (r, 0, 0))
    return pl.pallas_call(
        cross_forward_kernel,
        grid_spec=pltpu.PrefetchScalarGridSpec(
            num_scalar_prefetch=2,
            grid=(rows,),
            in_specs=[by_row(width), by_row(width), by_row(LANES), by_items(width, LANES)],
            out_specs=[by_items(LANES, width), by_items(heads, LANES)],
            scratch_shapes=[
                pltpu.VMEM((width // PAIR, 2 * LANES, 2 * LANES), BF),
                pltpu.VMEM((tiles_most, TILE, heads * LANES), F32),
                pltpu.VMEM((width // PAIR, PAIR, 2 * LANES), F32),
            ],
        ),
        out_shape=[
            jax.ShapeDtypeStruct((rows * items, LANES, width), F32),
            jax.ShapeDtypeStruct((rows * items, heads, LANES), F32),
        ],
        compiler_params=pltpu.CompilerParams(vmem_limit_bytes=48 << 20),
        cost_estimate=pl.CostEstimate(flops=rows * 19 * 4 * 512 * TILE * 1024, bytes_accessed=keys.shape[0] * 2304, transcendentals=0),
        name="cross_forward",
    )(layout["starts"], layout["ends"], keys, values, gate, qt)


def cross_backward_kernel(
    own_columns, first_ref, last_ref, mine_ref,
    memory_ref, memory_in_ref, keys_ref, values_ref, gate_ref,
    q_ref, qt_ref, g_ref, gt_ref, lse_ref, inner_ref, wk_ref, wv_ref,
    gmem_ref, dq_ref, dwk_ref, dwv_ref, dbv_ref,
    score_right, prob_right, key_right, value_right, dq_acc, dk_acc, dv_acc, low_k, low_v, wk_acc, wv_acc, bv_acc,
):
    row, tile = pl.program_id(0), pl.program_id(1)
    rows, tiles = pl.num_programs(0), pl.num_programs(1)
    step = row * tiles + tile
    width = keys_ref.shape[1]
    pairs = width // PAIR
    items = q_ref.shape[0]

    @pl.when(step == 0)
    def _():
        wk_acc[...] = jnp.zeros_like(wk_acc)
        wv_acc[...] = jnp.zeros_like(wv_acc)
        bv_acc[...] = jnp.zeros_like(bv_acc)

    @pl.when(tile == 0)
    def _():
        def lay_out(item, carry):
            for pair in range(pairs):
                columns = slice(pair * PAIR, (pair + 1) * PAIR)
                score_right[item, pair, :PAIR, :] = block_rows(qt_ref[item, columns, :])
                prob_right[item, pair, :PAIR, :] = block_rows(gt_ref[item, columns, :])
                lse = jnp.concatenate([lse_ref[item, 2 * pair : 2 * pair + 1, :], lse_ref[item, 2 * pair + 1 : 2 * pair + 2, :]], axis=1)
                inner = jnp.concatenate([inner_ref[item, 2 * pair : 2 * pair + 1, :], inner_ref[item, 2 * pair + 1 : 2 * pair + 2, :]], axis=1)
                score_right[item, pair, PAIR:, :] = gate_rows(item, items, FAR, -lse)
                prob_right[item, pair, PAIR:, :] = gate_rows(item, items, 0.0, -inner)
                key_right[item, pair] = block_columns(q_ref[item, :, columns])
                value_right[item, pair] = block_columns(g_ref[item, :, columns])
            return carry

        lax.fori_loop(0, items, lay_out, 0)
        dq_acc[...] = jnp.zeros_like(dq_acc)

    dk_acc[...] = jnp.zeros_like(dk_acc)
    dv_acc[...] = jnp.zeros_like(dv_acc)
    gate = gate_ref[...]

    def one_item(item, carry):
        for pair in range(pairs):
            columns = slice(pair * PAIR, (pair + 1) * PAIR)
            keys, values = keys_ref[:, columns], values_ref[:, columns]
            probs = jnp.exp(mm(jnp.concatenate([keys, gate], axis=1), score_right[item, pair]))
            slopes = mm(jnp.concatenate([values, gate], axis=1), prob_right[item, pair])
            low_probs = probs.astype(BF)
            low_scores = (probs * slopes).astype(BF)
            dv_acc[:, columns] += mm(low_probs, value_right[item, pair])
            dk_acc[:, columns] += mm(low_scores, key_right[item, pair])
            dq_acc[item, pair] += mm_tn(keys, low_scores)
        return carry

    lax.fori_loop(first_ref[step], last_ref[step] + 1, one_item, 0)
    grad_keys = dk_acc[...].astype(BF)
    grad_values = dv_acc[...].astype(BF)
    low_k[...] = grad_keys
    low_v[...] = grad_values
    gmem_ref[...] = mm_nt(grad_keys, wk_ref[...]) + mm_nt(grad_values, wv_ref[...])
    if own_columns == width:
        own = slice(None)
    else:
        own = pl.ds(pl.multiple_of(mine_ref[0] * own_columns, own_columns), own_columns)
    own_keys, own_values = low_k[:, own], low_v[:, own]
    wk_acc[...] += mm_tn(own_keys, memory_in_ref[...])
    wv_acc[...] += mm_tn(own_values, memory_ref[...])
    bv_acc[...] += jnp.sum(own_values.astype(F32).reshape(TILE // 8, 8, own_columns), axis=0)

    @pl.when(tile == tiles - 1)
    def _():
        def give(item, carry):
            parts = []
            for pair in range(pairs):
                both = dq_acc[item, pair]
                parts += [both[:HEAD, :LANES], both[HEAD:, LANES:]]
            dq_ref[item] = jnp.transpose(jnp.concatenate(parts, axis=0) * (1.0 / math.sqrt(HEAD))).astype(BF)
            return carry

        lax.fori_loop(0, items, give, 0)

    @pl.when(step == rows * tiles - 1)
    def _():
        dwk_ref[...] = jnp.transpose(wk_acc[...])
        dwv_ref[...] = jnp.transpose(wv_acc[...])
        dbv_ref[...] = jnp.sum(bv_acc[...], axis=0, keepdims=True)


def cross_backward(memory, memory_in, keys, values, gate, q, qt, g, gt, lse, inner, wk, wv, layout, own_columns, mine):
    rows, items, tiles = layout["rows"], layout["items"], layout["tiles"]
    total, feature = memory.shape
    width = keys.shape[1]
    heads, pairs = width // HEAD, width // PAIR
    slab = lambda columns: pl.BlockSpec((TILE, columns), lambda r, t, *_: (r * tiles + t, 0))
    whole = lambda shape: pl.BlockSpec(shape, lambda r, t, *_: (0,) * len(shape))
    by_items = lambda one, two: pl.BlockSpec((items, one, two), lambda r, t, *_: (r, 0, 0))
    return pl.pallas_call(
        functools.partial(cross_backward_kernel, own_columns),
        grid_spec=pltpu.PrefetchScalarGridSpec(
            num_scalar_prefetch=3,
            grid=(rows, tiles),
            in_specs=[
                slab(feature), slab(feature), slab(width), slab(width), slab(LANES),
                by_items(LANES, width), by_items(width, LANES), by_items(LANES, width), by_items(width, LANES),
                by_items(heads, LANES), by_items(heads, LANES),
                whole(wk.shape), whole(wv.shape),
            ],
            out_specs=[
                slab(feature), by_items(LANES, width),
                whole((feature, own_columns)), whole((feature, own_columns)), whole((1, own_columns)),
            ],
            scratch_shapes=[
                pltpu.VMEM((items, pairs, 2 * LANES, 2 * LANES), BF),
                pltpu.VMEM((items, pairs, 2 * LANES, 2 * LANES), BF),
                pltpu.VMEM((items, pairs, 2 * LANES, PAIR), BF),
                pltpu.VMEM((items, pairs, 2 * LANES, PAIR), BF),
                pltpu.VMEM((items, pairs, PAIR, 2 * LANES), F32),
                pltpu.VMEM((TILE, width), F32),
                pltpu.VMEM((TILE, width), F32),
                pltpu.VMEM((TILE, width), BF),
                pltpu.VMEM((TILE, width), BF),
                pltpu.VMEM((own_columns, feature), F32),
                pltpu.VMEM((own_columns, feature), F32),
                pltpu.VMEM((8, own_columns), F32),
            ],
        ),
        out_shape=[
            jax.ShapeDtypeStruct((total, feature), F32),
            jax.ShapeDtypeStruct((rows * items, LANES, width), BF),
            jax.ShapeDtypeStruct((feature, own_columns), F32),
            jax.ShapeDtypeStruct((feature, own_columns), F32),
            jax.ShapeDtypeStruct((1, own_columns), F32),
        ],
        compiler_params=pltpu.CompilerParams(vmem_limit_bytes=48 << 20),
        cost_estimate=pl.CostEstimate(flops=60 * total * feature * width // 4, bytes_accessed=total * 6144, transcendentals=0),
        name="cross_backward",
    )(
        layout["first"], layout["last"], mine, memory, memory_in, keys, values, gate,
        q, qt, g, gt, lse, inner, wk, wv,
    )


def position_tables(starts, tiles, feature):
    lane = jnp.arange(feature, dtype=jnp.int32)
    rates = jnp.exp((lane // 2).astype(F32) * (-2.0 * math.log(10000.0) / feature))
    turn = jnp.where(lane % 2 == 1, 0.5 * math.pi, 0.0).astype(F32)
    local = jnp.arange(TILE, dtype=F32)[:, None] * rates[None, :]
    begin = TILE * jnp.arange(tiles, dtype=jnp.int32)[None, :, None] - starts[:, None, :]
    angle = begin.astype(F32).reshape(-1, starts.shape[1])[:, :, None] * rates + turn
    return {"tile_sin": jnp.sin(angle), "tile_cos": jnp.cos(angle), "local_sin": jnp.sin(local), "local_cos": jnp.cos(local)}


def memory_layout(lengths, key_pad):
    rows, items = lengths.shape
    slots = key_pad.shape[1]
    tiles = slots // TILE
    ends = jnp.cumsum(lengths, axis=1).astype(jnp.int32)
    starts = (ends - lengths).astype(jnp.int32)
    base = TILE * jnp.arange(tiles, dtype=jnp.int32)
    first = jnp.sum((ends[:, None, :] <= base[None, :, None]).astype(jnp.int32), axis=2)
    last = jnp.sum((starts[:, None, :] < base[None, :, None] + TILE).astype(jnp.int32), axis=2) - 1
    bounds = jnp.pad(jnp.stack([starts, ends], axis=1), ((0, 0), (0, 0), (0, LANES - items)))
    return {
        "rows": rows, "items": items, "slots": slots, "tiles": tiles, "longest": 1200,
        "starts": starts, "ends": ends, "first": first.reshape(-1), "last": last.reshape(-1),
        "bounds": bounds, "pad": key_pad.reshape(rows * tiles, 1, TILE),
    }


def layer_norm(value_in, norm_gain, norm_shift):
    center = value_in - jnp.mean(value_in, axis=-1, keepdims=True)
    spread = jnp.mean(center * center, axis=-1, keepdims=True)
    return center * lax.rsqrt(spread + 1e-05) * norm_gain + norm_shift


def smooth_act(pre_act):
    return 0.5 * pre_act * (1.0 + jnp.tanh(math.sqrt(2.0 / math.pi) * (pre_act + 0.044715 * pre_act * pre_act * pre_act)))


def column_sums(matrix):
    return jnp.sum(matrix.astype(F32), axis=0)


def self_forward(queries, keys_in, values_in):
    scores = jnp.einsum("iqhe,ikhe->ihqk", queries, keys_in, preferred_element_type=F32) / math.sqrt(HEAD)
    largest = jnp.max(scores, axis=-1, keepdims=True)
    expo = jnp.exp(scores - largest)
    probs = expo / jnp.sum(expo, axis=-1, keepdims=True)
    mix = jnp.einsum("ihqk,ikhe->iqhe", probs.astype(BF), values_in, preferred_element_type=F32)
    return mix.astype(BF), probs


def self_backward(queries, keys_in, values_in, probs, grad_mixed):
    grad_values = jnp.einsum("ihqk,iqhe->ikhe", probs.astype(BF), grad_mixed, preferred_element_type=F32)
    grad_probs = jnp.einsum("iqhe,ikhe->ihqk", grad_mixed, values_in, preferred_element_type=F32)
    inner = jnp.sum(grad_probs * probs, axis=-1, keepdims=True)
    grad_scores = (probs * (grad_probs - inner)).astype(BF)
    grad_queries = jnp.einsum("ihqk,ikhe->iqhe", grad_scores, keys_in, preferred_element_type=F32) / math.sqrt(HEAD)
    grad_keys = jnp.einsum("ihqk,iqhe->ikhe", grad_scores, queries, preferred_element_type=F32) / math.sqrt(HEAD)
    return grad_queries.astype(BF), grad_keys.astype(BF), grad_values.astype(BF)


def solution(mesh):
    tensor = mesh.shape["tensor"]

    def body(
        tokens, memory, mem_lengths, key_pad, query_embed,
        self_wq, self_bq, self_wk, self_wv, self_bv, self_wo, self_bo, norm1_gain, norm1_bias,
        cross_wq, cross_bq, cross_wk, cross_wv, cross_bv, cross_wo, cross_bo, norm2_gain, norm2_bias,
        ffn_w1, ffn_b1, ffn_w2, ffn_b2, norm3_gain, norm3_bias, cotangent,
    ):
        mine = lax.axis_index("tensor")
        own_columns = self_wq.shape[1]
        own_hidden = ffn_w1.shape[1]

        def whole(part, dim):
            if tensor == 1:
                return part
            if tensor != 2:
                return lax.all_gather(part, "tensor", axis=dim, tiled=True)
            other = lax.ppermute(part, "tensor", [(0, 1), (1, 0)])
            low, high = jnp.where(mine == 0, part, other), jnp.where(mine == 0, other, part)
            return jnp.concatenate([low, high], axis=dim)

        def own(full, dim, size):
            return lax.dynamic_slice_in_dim(full, mine * size, size, axis=dim)

        token_count, feature = tokens.shape
        row_count = mem_lengths.shape[0]
        items = token_count // SPAN
        width = own_columns * tensor
        heads = width // HEAD
        to_items = lambda matrix: matrix.reshape(items, SPAN, heads, HEAD)
        padded = lambda matrix: jnp.pad(matrix.reshape(items, SPAN, -1), ((0, 0), (0, LANES - SPAN), (0, 0)))

        swq, swk, swv, swo = whole(self_wq, 1), whole(self_wk, 1), whole(self_wv, 1), whole(self_wo, 0)
        sbq, sbv = whole(self_bq, 0), whole(self_bv, 0)
        cwk, cwv, cbv = whole(cross_wk, 1), whole(cross_wv, 1), whole(cross_bv, 0)
        cwq, cwo, cbq = whole(cross_wq, 1), whole(cross_wo, 0), whole(cross_bq, 0)
        w1, w2, b1 = whole(ffn_w1, 1), whole(ffn_w2, 0), whole(ffn_b1, 0)

        layout = memory_layout(mem_lengths, key_pad)
        tables = position_tables(layout["starts"], layout["tiles"], feature)
        memory_in, cross_keys, cross_values, gate = keys_values(memory, layout, tables, cwk, cwv, cbv[None, :])

        query_pos = jnp.tile(query_embed, (items, 1))
        tokens_wide = tokens.astype(F32)
        shared_in = (tokens_wide + query_pos).astype(BF)
        self_query = (mm(shared_in, swq) + sbq).astype(BF)
        self_keys = mm(shared_in, swk).astype(BF)
        self_values = (mm(tokens, swv) + sbv).astype(BF)
        self_mix, self_probs = self_forward(to_items(self_query), to_items(self_keys), to_items(self_values))
        self_mix = self_mix.reshape(token_count, width)
        resid_one = tokens_wide + (mm(self_mix, swo) + self_bo)
        normed_one, pull_one = jax.vjp(layer_norm, resid_one, norm1_gain, norm1_bias)
        cross_in = (normed_one + query_pos).astype(BF)
        cross_query = (mm(cross_in, cwq) + cbq).astype(BF)
        q = padded(cross_query * jnp.asarray(1.0 / math.sqrt(HEAD), BF))
        qt = jnp.swapaxes(q, 1, 2)
        mix, lse = cross_forward(cross_keys, cross_values, gate, qt, layout)
        mix_wide = mix[:, :SPAN].reshape(token_count, width)
        cross_mix = mix_wide.astype(BF)
        resid_two = normed_one + (mm(cross_mix, cwo) + cross_bo)
        normed_two, pull_two = jax.vjp(layer_norm, resid_two, norm2_gain, norm2_bias)
        ffn_input = normed_two.astype(BF)
        pre_act = mm(ffn_input, w1) + b1
        hidden_wide, pull_act = jax.vjp(smooth_act, pre_act)
        hidden = hidden_wide.astype(BF)
        resid_three = normed_two + (mm(hidden, w2) + ffn_b2)
        normed_three, pull_three = jax.vjp(layer_norm, resid_three, norm3_gain, norm3_bias)
        layer_out = normed_three.astype(BF)
        grad_three, grad_norm3_gain, grad_norm3_bias = pull_three(cotangent.astype(F32))
        low_three = grad_three.astype(BF)
        grad_ffn_b2 = column_sums(low_three)
        grad_ffn_w2 = mm_tn(own(hidden, 1, own_hidden), low_three)
        (grad_pre,) = pull_act(mm_nt(low_three, w2))
        low_pre = grad_pre.astype(BF)
        own_pre = own(low_pre, 1, own_hidden)
        grad_ffn_b1 = column_sums(own_pre)
        grad_ffn_w1 = mm_tn(ffn_input, own_pre)
        grad_two, grad_norm2_gain, grad_norm2_bias = pull_two(grad_three + mm_nt(low_pre, w1))
        low_two = grad_two.astype(BF)
        grad_cross_bo = column_sums(low_two)
        grad_cross_wo = mm_tn(own(cross_mix, 1, own_columns), low_two)
        grad_cross_mix = mm_nt(low_two, cwo).astype(BF)
        inner = jnp.sum((grad_cross_mix.astype(F32) * mix_wide).reshape(items, SPAN, heads, HEAD), axis=-1)
        inner = jnp.pad(jnp.swapaxes(inner, 1, 2), ((0, 0), (0, 0), (0, LANES - SPAN)))
        g = padded(grad_cross_mix)
        gt = jnp.swapaxes(g, 1, 2)
        kernel_columns = own_columns if own_columns % LANES == 0 else width
        grad_memory, dq, grad_cross_wk, grad_cross_wv, grad_cross_bv = cross_backward(
            memory, memory_in, cross_keys, cross_values, gate, q, qt, g, gt, lse, inner, cwk, cwv,
            layout, kernel_columns, mine[None].astype(jnp.int32),
        )
        grad_cross_bv = grad_cross_bv[0]
        if kernel_columns != own_columns:
            grad_cross_wk, grad_cross_wv = own(grad_cross_wk, 1, own_columns), own(grad_cross_wv, 1, own_columns)
            grad_cross_bv = own(grad_cross_bv, 0, own_columns)
        grad_cross_query = dq[:, :SPAN].reshape(token_count, width)
        own_query = own(grad_cross_query, 1, own_columns)
        grad_cross_bq = column_sums(own_query)
        grad_cross_wq = mm_tn(cross_in, own_query)
        grad_cross_in = mm_nt(grad_cross_query, cwq)
        grad_one, grad_norm1_gain, grad_norm1_bias = pull_one(grad_two + grad_cross_in)
        low_one = grad_one.astype(BF)
        grad_self_bo = column_sums(low_one)
        grad_self_wo = mm_tn(own(self_mix, 1, own_columns), low_one)
        grad_self_mix = mm_nt(low_one, swo).astype(BF)
        grad_self_query, grad_self_keys, grad_self_values = self_backward(
            to_items(self_query), to_items(self_keys), to_items(self_values), self_probs, to_items(grad_self_mix)
        )
        grad_self_query = grad_self_query.reshape(token_count, width)
        grad_self_keys = grad_self_keys.reshape(token_count, width)
        grad_self_values = grad_self_values.reshape(token_count, width)
        own_sq, own_sk, own_sv = (own(one, 1, own_columns) for one in (grad_self_query, grad_self_keys, grad_self_values))
        grad_self_bq = column_sums(own_sq)
        grad_self_wq = mm_tn(shared_in, own_sq)
        grad_self_wk = mm_tn(shared_in, own_sk)
        grad_self_wv = mm_tn(tokens, own_sv)
        grad_self_bv = column_sums(own_sv)
        grad_shared = mm_nt(grad_self_query, swq) + mm_nt(grad_self_keys, swk)
        grad_tokens = grad_one + grad_shared + mm_nt(grad_self_values, swv)
        grad_query_embed = jnp.sum((grad_shared + grad_cross_in).reshape(items, SPAN, feature), axis=0)
        partial = [
            grad_query_embed, grad_self_wq, grad_self_bq, grad_self_wk, grad_self_wv, grad_self_bv, grad_self_wo, grad_self_bo,
            grad_norm1_gain, grad_norm1_bias, grad_cross_wq, grad_cross_bq, grad_cross_wk, grad_cross_wv, grad_cross_bv,
            grad_cross_wo, grad_cross_bo, grad_norm2_gain, grad_norm2_bias, grad_ffn_w1, grad_ffn_b1, grad_ffn_w2, grad_ffn_b2,
            grad_norm3_gain, grad_norm3_bias,
        ]
        out = [lax.psum(one.astype(BF), "dp").astype(F32) for one in partial]
        return (layer_out, grad_tokens, grad_memory, *out)

    rep, by_row, by_col, by_first = P(), P("dp", None), P(None, "tensor"), P("tensor", None)
    one_dim = P("tensor")
    return jax.shard_map(
        body,
        mesh=mesh,
        in_specs=(
            by_row, by_row, by_row, by_row, rep,
            by_col, one_dim, by_col, by_col, one_dim, by_first, rep, rep, rep,
            by_col, one_dim, by_col, by_col, one_dim, by_first, rep, rep, rep,
            by_col, one_dim, by_first, rep, rep, rep, by_row,
        ),
        out_specs=(
            by_row, by_row, by_row, rep,
            by_col, one_dim, by_col, by_col, one_dim, by_first, rep, rep, rep,
            by_col, one_dim, by_col, by_col, one_dim, by_first, rep, rep, rep,
            by_col, one_dim, by_first, rep, rep, rep,
        ),
        check_vma=False,
    )
```

time: 1190 us -> 526 us (0.44)
  waiting for transfers between devices: 432 us -> 64.1 us
  matrix products: 293 us -> 93 us
  Pallas kernels: 0 us -> 134 us
  local copies, waits for them, and re-layouts: 205 us -> 76 us
  other arithmetic: 169 us -> 56.5 us
  starting transfers between devices: 1.16 us -> 17.3 us
    psum x7 -> x1, waiting for transfers between devices: 432 us -> 57.8 us  [body(): out = [lax.psum(one.astype(BF), 'dp').astype(F32) for one in partial]]
    dot_general x49 -> x29, matrix products: 290 us -> 88.1 us  [the longest x8 34.7 us: mm_nt(): lax.dot_general(left, right, (((1,), (1,)), ((), ())), preferred_element_...]
    pallas_call x0 -> x3, Pallas kernels: none -> 134 us  [the longest x1 71.6 us: cross_backward(): pl.pallas_call(functools.partial(cross_backward_kernel, own_columns), gri...]
    while x28 -> x0, local copies, waits for them, and re-layouts: 54 us -> none  [the longest x4 28.7 us: body(): lax.map(cross_row, (to_rows(cross_query, query_count), to_rows(cross_keys...]
    convert_element_type x30 -> x32, other arithmetic: 70.4 us -> 25.8 us  [the longest x27 22 us: body(): out = [lax.psum(one.astype(BF), 'dp').astype(F32) for one in partial]]
    reshape x21 -> x22, local copies, waits for them, and re-layouts: 73.4 us -> 36.6 us  [the longest x8 17 us: body(): to_items = lambda matrix: matrix.reshape(items, SPAN, heads, HEAD)]
    sin x1 -> x0, other arithmetic: 29.9 us -> none  [sinusoid(): jnp.sin(angles)]
    another operation x9 -> x2, local copies, waits for them, and re-layouts: 31.6 us -> 3.86 us  [body(): query_pos = jnp.tile(query_embed, (items, 1))]
  transfers between devices with their start and end apart: 7 -> 16, of which waited for: 6 -> 3; matrix products, arithmetic and copies ran while one was open for 20% -> 17% of each run, Pallas kernels for 0% -> 12%
where the time goes in v1:
time: 526 us; the launch traced here: 516 us
  Pallas kernels  134 us (25%)
  matrix products  93 us (18%)
  local copies, waits for them, and re-layouts  76 us (14%)
  waiting for transfers between devices  64.1 us (12%)
  blocking collectives  59.9 us (11%)
  other arithmetic  56.5 us (11%)
  starting transfers between devices  17.3 us (3%)
  between operations  15.7 us (3%)
    pallas_call x1, Pallas kernels, cross_backward(): pl.pallas_call(functools.partial(cross_backward_kernel, own_columns), gri...  71.6 us
    psum x1, blocking collectives, body(): out = [lax.psum(one.astype(BF), 'dp').astype(F32) for one in partial]  59.9 us
    psum x1, waiting for transfers between devices, body(): out = [lax.psum(one.astype(BF), 'dp').astype(F32) for one in partial]  57.8 us
    dot_general x8, matrix products, mm_nt(): lax.dot_general(left, right, (((1,), (1,)), ((), ())), preferred_element_...  34.7 us
    pallas_call x1, Pallas kernels, keys_values(): pl.pallas_call(keys_values_kernel, grid_spec=pltpu.PrefetchScalarGridSpec...  31.3 us
    pallas_call x1, Pallas kernels, cross_forward(): pl.pallas_call(cross_forward_kernel, grid_spec=pltpu.PrefetchScalarGridSp...  31 us
    unnamed x201, local copies, waits for them, and re-layouts  23 us
    convert_element_type x27, other arithmetic, body(): out = [lax.psum(one.astype(BF), 'dp').astype(F32) for one in partial]  22 us
  transfers between devices with their start and end apart: 16, of which 3 were waited for; matrix products, arithmetic and copies ran while one was open for 17% of the time, Pallas kernels for 12%

profile of v1, /device:TPU:0, one launch (start us, length us, event | category | flops | bytes accessed | tf_op | source)
XLA Modules:
  0.0 516.4 jit_solution(13175528455796608470)
XLA Ops:
  7.2 3.0 collective-permute-start.1
  23.3 2.9 fusion.41
  32.2 4.8 collective-permute-done.13
  66.4 5.0 fusion.94
  90.7 31.3 %keys_values.1 = (bf16[8192,512]{1,0:T(8,128)(2,1)S(1)}, bf16[8192,512]{1,0:T(8,128)(2,1)}, bf16[8192,512]{1,0:T(8,128)(2,1)}, bf16[8192,128]{1,0:T(8,128)(2,1)S(1)}) custom-call(s32[32]{0:T(128)S(1)} %reshape.301.first_ref, s32[32]{0:T(128)S(1)} %sub.87.last_ref, s32[2,4]{1,0:T(2,128)S(1)} %sub.85.starts_ref, s32[2,4]{1,0:T(2,128)S(1)} %reduce_window_sum.11.ends_ref, ...), custom_call_target="tpu_custom_call" | custom-call | flops 8589934592 | bytes 33554432 | tf_op jit(solution)/shard_map/keys_values/pallas_call | solution.py:89
  122.1 3.3 copy-done.5
  125.3 31.0 %cross_forward.1 = (f32[8,128,512]{2,1,0:T(8,128)S(1)}, f32[8,8,128]{2,1,0:T(8,128)S(1)}) custom-call(s32[2,4]{1,0:T(2,128)S(1)} %sub.85.starts_ref, s32[2,4]{1,0:T(2,128)S(1)} %reduce_window_sum.11.ends_ref, bf16[8192,512]{1,0:T(8,128)(2,1)} %get-tuple-element.39.keys_ref, bf16[8192,512]{1,0:T(8,128)(2,1)} %get-tuple-element.40.values_ref, ...), custom_call_target="tpu_custom_call" | custom-call | flops 20401094656 | bytes 18874368 | tf_op jit(solution)/shard_map/cross_forward/pallas_call | solution.py:209
  170.6 8.7 %multiply_convert_fusion = (bf16[800,3200]{1,0:T(8,128)(2,1)S(1)}, f32[800,3200]{1,0:T(8,128)}) fusion(f32[3200]{0:T(1024)S(1)} %pad_maximum_fusion.30, bf16[512,1600]{0,1:T(8,128)(2,1)S(1)} %get-tuple-element.211, bf16[512,1600]{0,1:T(8,128)(2,1)S(1)} %get-tuple-element.210, f32[800,512]{1,0:T(8,128)S(1)} %get-tuple-element.248, f32[512]{0:T(512)S(1)} %copy-done.98, ...), kind=kOutput, calls=%fused_computation.11 | convolution fusion | flops 2655641600 | bytes 20298496 | tf_op jit(solution)/shard_map/dot_general | solution.py:23
  181.0 3.2 fusion.97
  187.9 4.6 convolution_convert_fusion
  192.5 14.3 %fusion.4 = bf16[800,3200]{1,0:T(8,128)(2,1)S(1)} fusion(f32[800,3200]{1,0:T(8,128)} %get-tuple-element.250, bf16[800,512]{1,0:T(8,128)(2,1)S(1)} %get-tuple-element.196, f32[3200]{0:T(1024)S(1)} %pad_maximum_fusion.30, bf16[1600,512]{1,0:T(8,128)(2,1)S(1)} %get-tuple-element.209, bf16[1600,512]{1,0:T(8,128)(2,1)S(1)} %get-tuple-element.208), kind=kOutput, calls=%fused_computation.8 | convolution fusion | flops 2691993600 | bytes 19468800 | tf_op jit(solution)/shard_map/dot_general | solution.py:31
  206.8 4.9 convolution_convert_fusion.1
  211.7 3.5 multiply_reduce_fusion.2
  230.6 3.3 reshape.306
  237.3 71.6 %cross_backward.1 = (f32[8192,512]{1,0:T(8,128)}, bf16[8,128,512]{2,1,0:T(8,128)(2,1)S(1)}, f32[512,256]{1,0:T(8,128)S(1)}, f32[512,256]{1,0:T(8,128)S(1)}, f32[1,256]{1,0:T(1,128)S(1)}) custom-call(s32[32]{0:T(128)S(1)} %reshape.301.first_ref, s32[32]{0:T(128)S(1)} %sub.87.last_ref, s32[1]{0:T(128)} %bitcast.8.mine_ref, bf16[8192,512]{1,0:T(8,128)(2,1)} %memory_ref.3, ...), custom_call_target="tpu_custom_call" | custom-call | flops 32212254720 | bytes 50331648 | tf_op jit(solution)/shard_map/cross_backward/pallas_call | solution.py:329
  311.9 3.6 multiply_reduce_fusion.3
  323.7 4.4 fusion.22
  334.9 2.9 fusion.40
  349.5 4.3 fusion.98
  363.4 3.1 dynamic-slice_reduce_fusion
  366.5 59.9 %all-reduce.4 = (bf16[256]{0:T(256)(128)(2,1)S(1)}, bf16[256]{0:T(256)(128)(2,1)S(1)}, bf16[512]{0:T(512)(128)(2,1)S(1)}, bf16[512]{0:T(512)(128)(2,1)S(1)}, bf1...) all-reduce(bf16[256]{0:T(256)(128)(2,1)S(1)} %dynamic-slice_reduce_, ...), channel_id=1, replica_groups=mesh['dp'=16,'tensor'=2] {'dp'}, use_global_device_ids=true, to_apply=%region_23.24 | all-reduce | flops 7232 | bytes 28928 | tf_op jit(solution)/shard_map/psum | solution.py:562
  434.5 3.4 add_add_fusion.3
  437.9 57.8 %all-reduce.8.cloned.1.call-done = (bf16[512,256]{0,1:T(8,128)(2,1)}, bf16[100,512]{1,0:T(8,128)(2,1)}, bf16[512,256]{1,0:T(8,128)(2,1)}, bf16[512,256]{1,0:T(8,...) async-done(((bf16[512,256]{0,1:T(8,128)(2,1)}, ...) | async-done | bytes 5476368 | tf_op jit(solution)/shard_map/psum | solution.py:562
  495.7 3.7 convert_element_type.341
  (379 shorter events, 162.4 us)
Async XLA Ops:
  7.2 488.5 %all-reduce.8.cloned.1.call-start = ((), (), s32[]{:S(2)}) async-start(), calls=%async_computation | async-start | bytes 10960896 | tf_op jit(solution)/shard_map/psum | solution.py:562
  7.2 19.2 %collective-permute-start.1 = (f32[256]{0:T(256)}, f32[256]{0:T(256)S(1)}, u32[]{:S(2)}, u32[]{:S(2)}) collective-permute-start(f32[256]{0:T(256)} %param.39), channel_id=1, source_target_pairs={{0,1},{1,0},{2,3},{3,2},{4,5},{5,4},{6,7},{7,6},{8,9},{9,8},{10,11... | collective-permute-start | bytes 3080 | tf_op jit(solution)/shard_map/ppermute | solution.py:453
  10.3 16.4 %collective-permute-start.3 = (f32[256]{0:T(256)}, f32[256]{0:T(256)S(1)}, u32[]{:S(2)}, u32[]{:S(2)}) collective-permute-start(f32[256]{0:T(256)} %param.36), channel_id=1, source_target_pairs={{0,1},{1,0},{2,3},{3,2},{4,5},{5,4},{6,7},{7,6},{8,9},{9,8},{10,11... | collective-permute-start | bytes 3080 | tf_op jit(solution)/shard_map/ppermute | solution.py:453
  10.3 28.0 %collective-permute-start.2 = (bf16[512,256]{1,0:T(8,128)(2,1)}, bf16[512,256]{1,0:T(8,128)(2,1)}, u32[]{:S(2)}, u32[]{:S(2)}) collective-permute-start(bf16[512,256]{1,0:T(8,128)(2,1)} %param.35), channel_id=1, source_target_pairs={{0,1},{1,0},{2,3},{3,2},{4,5},{5,4},{6,7},{7,6},{8,9},{9,8},{10,11... | collective-permute-start | bytes 786440 | tf_op jit(solution)/shard_map/ppermute | solution.py:453
  12.3 34.4 %collective-permute-start.4 = (bf16[512,256]{1,0:T(8,128)(2,1)}, bf16[512,256]{1,0:T(8,128)(2,1)}, u32[]{:S(2)}, u32[]{:S(2)}) collective-permute-start(bf16[512,256]{1,0:T(8,128)(2,1)} %param.37), channel_id=1, source_target_pairs={{0,1},{1,0},{2,3},{3,2},{4,5},{5,4},{6,7},{7,6},{8,9},{9,8},{10,11... | collective-permute-start | bytes 786440 | tf_op jit(solution)/shard_map/ppermute | solution.py:453
  12.4 44.4 %collective-permute-start = (bf16[512,256]{1,0:T(8,128)(2,1)}, bf16[512,256]{1,0:T(8,128)(2,1)}, u32[]{:S(2)}, u32[]{:S(2)}) collective-permute-start(bf16[512,256]{1,0:T(8,128)(2,1)} %param.38), channel_id=1, source_target_pairs={{0,1},{1,0},{2,3},{3,2},{4,5},{5,4},{6,7},{7,6},{8,9},{9,8},{10,11... | collective-permute-start | bytes 786440 | tf_op jit(solution)/shard_map/ppermute | solution.py:453
  20.9 10.4 %copy-start.85 = (f32[1600]{0:T(1024)S(1)}, f32[1600]{0:T(1024)}, u32[]{:S(2)}) copy-start(f32[1600]{0:T(1024)} %param.54) | copy-start | bytes 19204
  21.0 18.1 %copy-start.74 = (bf16[512,256]{1,0:T(8,128)(2,1)S(1)}, bf16[512,256]{1,0:T(8,128)(2,1)}, u32[]{:S(2)}) copy-start(bf16[512,256]{1,0:T(8,128)(2,1)} %param.35) | copy-start | bytes 786436
  23.3 17.6 %copy-start.57 = (bf16[800,512]{1,0:T(8,128)(2,1)S(1)}, bf16[800,512]{1,0:T(8,128)(2,1)}, u32[]{:S(2)}) copy-start(bf16[800,512]{1,0:T(8,128)(2,1)} %fusion.19) | copy-start | bytes 2457604
  26.5 3.6 collective-permute-start.10
  26.6 4.7 collective-permute-start.8
  30.1 46.5 %collective-permute-start.11 = (bf16[256,512]{1,0:T(8,128)(2,1)}, bf16[256,512]{1,0:T(8,128)(2,1)}, u32[]{:S(2)}, u32[]{:S(2)}) collective-permute-start(bf16[256,512]{1,0:T(8,128)(2,1)} %param.49), channel_id=1, source_target_pairs={{0,1},{1,0},{2,3},{3,2},{4,5},{5,4},{6,7},{7,6},{8,9},{9,8},{10,11... | collective-permute-start | bytes 786440 | tf_op jit(solution)/shard_map/ppermute | solution.py:453
  31.3 5.6 %collective-permute-start.13 = (f32[1600]{0:T(1024)S(1)}, f32[1600]{0:T(1024)S(1)}, u32[]{:S(2)}, u32[]{:S(2)}) collective-permute-start(f32[1600]{0:T(1024)S(1)} %copy-done.85), channel_id=1, source_target_pairs={{0,1},{1,0},{2,3},{3,2},{4,5},{5,4},{6,7},{7,6},{8,9},{9,8},{10,11... | collective-permute-start | bytes 19208 | tf_op jit(solution)/shard_map/ppermute | solution.py:453
  36.9 41.0 %collective-permute-start.5 = (bf16[256,512]{1,0:T(8,128)(2,1)}, bf16[256,512]{1,0:T(8,128)(2,1)}, u32[]{:S(2)}, u32[]{:S(2)}) collective-permute-start(bf16[256,512]{1,0:T(8,128)(2,1)} %param.40), channel_id=1, source_target_pairs={{0,1},{1,0},{2,3},{3,2},{4,5},{5,4},{6,7},{7,6},{8,9},{9,8},{10,11... | collective-permute-start | bytes 786440 | tf_op jit(solution)/shard_map/ppermute | solution.py:453
  38.4 45.5 %collective-permute-start.9 = (bf16[512,256]{1,0:T(8,128)(2,1)}, bf16[512,256]{1,0:T(8,128)(2,1)}, u32[]{:S(2)}, u32[]{:S(2)}) collective-permute-start(bf16[512,256]{1,0:T(8,128)(2,1)} %param.44), channel_id=1, source_target_pairs={{0,1},{1,0},{2,3},{3,2},{4,5},{5,4},{6,7},{7,6},{8,9},{9,8},{10,11... | collective-permute-start | bytes 786440 | tf_op jit(solution)/shard_map/ppermute | solution.py:453
  46.7 42.5 %collective-permute-start.6 = (bf16[512,256]{1,0:T(8,128)(2,1)}, bf16[512,256]{1,0:T(8,128)(2,1)}, u32[]{:S(2)}, u32[]{:S(2)}) collective-permute-start(bf16[512,256]{1,0:T(8,128)(2,1)} %param.46), channel_id=1, source_target_pairs={{0,1},{1,0},{2,3},{3,2},{4,5},{5,4},{6,7},{7,6},{8,9},{9,8},{10,11... | collective-permute-start | bytes 786440 | tf_op jit(solution)/shard_map/ppermute | solution.py:453
  56.8 32.4 %collective-permute-start.7 = (bf16[512,256]{1,0:T(8,128)(2,1)}, bf16[512,256]{1,0:T(8,128)(2,1)}, u32[]{:S(2)}, u32[]{:S(2)}) collective-permute-start(bf16[512,256]{1,0:T(8,128)(2,1)} %param.47), channel_id=1, source_target_pairs={{0,1},{1,0},{2,3},{3,2},{4,5},{5,4},{6,7},{7,6},{8,9},{9,8},{10,11... | collective-permute-start | bytes 786440 | tf_op jit(solution)/shard_map/ppermute | solution.py:453
  76.6 91.3 %collective-permute-start.12 = (bf16[512,1600]{0,1:T(8,128)(2,1)}, bf16[512,1600]{0,1:T(8,128)(2,1)}, u32[]{:S(2)}, u32[]{:S(2)}) collective-permute-start(bf16[512,1600]{0,1:T(8,128)(2,1)} %param.53), channel_id=1, source_target_pairs={{0,1},{1,0},{2,3},{3,2},{4,5},{5,4},{6,7},{7,6},{8,9},{9,8},{10,11... | collective-permute-start | bytes 4915208 | tf_op jit(solution)/shard_map/ppermute | solution.py:453
  77.9 101.4 %collective-permute-start.14 = (bf16[1600,512]{1,0:T(8,128)(2,1)}, bf16[1600,512]{1,0:T(8,128)(2,1)}, u32[]{:S(2)}, u32[]{:S(2)}) collective-permute-start(bf16[1600,512]{1,0:T(8,128)(2,1)} %param.55), channel_id=1, source_target_pairs={{0,1},{1,0},{2,3},{3,2},{4,5},{5,4},{6,7},{7,6},{8,9},{9,8},{10,11... | collective-permute-start | bytes 4915208 | tf_op jit(solution)/shard_map/ppermute | solution.py:453
  90.7 31.4 %copy-start = (bf16[512,512]{1,0:T(8,128)(2,1)}, bf16[512,512]{1,0:T(8,128)(2,1)S(1)}, u32[]{:S(2)}) copy-start(bf16[512,512]{1,0:T(8,128)(2,1)S(1)} %pad_maximum_fusion.14.wk_ref) | copy-start | bytes 1572868
  90.7 31.3 %copy-start.2 = (bf16[512,512]{1,0:T(8,128)(2,1)}, bf16[512,512]{1,0:T(8,128)(2,1)S(1)}, u32[]{:S(2)}) copy-start(bf16[512,512]{1,0:T(8,128)(2,1)S(1)} %pad_maximum_fusion.15.wv_ref) | copy-start | bytes 1572868
  362.1 72.4 %copy-start.14 = (f32[800,512]{1,0:T(8,128)S(1)}, f32[800,512]{1,0:T(8,128)}, u32[]{:S(2)}) copy-start(f32[800,512]{1,0:T(8,128)} %copy-done.13) | copy-start | bytes 4915204
  362.1 72.4 %copy-start.39 = (bf16[512,256]{1,0:T(8,128)(2,1)S(1)}, bf16[512,256]{1,0:T(8,128)(2,1)}, u32[]{:S(2)}) copy-start(bf16[512,256]{1,0:T(8,128)(2,1)} %copy-done.38) | copy-start | bytes 786436
  362.1 72.4 %copy-start.41 = (bf16[512,256]{1,0:T(8,128)(2,1)S(1)}, bf16[512,256]{1,0:T(8,128)(2,1)}, u32[]{:S(2)}) copy-start(bf16[512,256]{1,0:T(8,128)(2,1)} %copy-done.40) | copy-start | bytes 786436
  (91 other events, 246.9 us)
Sparse Core Ops, SparseCore 0:
  360.6 135.1 all-reduce.7
